TPU v7x, 256 devices: a whole 4x4x8 slice. The times are simulated.
256 devices in a mesh: band: 32 (over z, x), gvec: 8 (over y, core).
Axes of the slice: x: 4, y: 4, z: 8, core: 2. Of those that a mesh axis runs over, the one named last changes fastest.
Arguments:
- pairs: bfloat16 [32, 8, 512, 640], P(None, 'gvec', 'band'), may hold values from -0.59765625 to 0.59765625
- cond_energy: float32 [512], replicated, may hold values from 0.5 to 12
- val_energy: float32 [32, 8], replicated, may hold values from -12 to -2
- band_counts: int32 [32], replicated, may hold values from 1 to 16, as said below
- slab: int32 [1], replicated, may hold values from 0 to 31
Outputs:
- chi_zero: float32 [20480, 20480], P('gvec', 'band')
Inputs may be any that keep to these rules, and one draw needn't show every extreme that they name: `band_counts`: every owner has at least one occupied slot, and in every draw some owner has all 16 slots occupied.
All inputs are finite; a program needn't handle non-finite values.
Results may differ from a plain program's by a relative error of at most 0.0028.
Values may be sent and summed in bfloat16 or wider, within the bound.
No kernel may reach another device: no remote copies, remote signals or barrier semaphores. Data moves between devices by JAX's collectives and lax.ppermute only.
A program may use at most 128 MiB of HBM per device.

v0:
```python
import jax
import jax.numpy as jnp
from jax import lax
from jax.sharding import PartitionSpec as P


def on_device(pairs, cond_energy, val_energy, band_counts, slab):
    n_band = lax.axis_size("band")
    n_gvec = lax.axis_size("gvec")
    ratio = n_band // n_gvec
    local_v = pairs.shape[1]
    slot_count = pairs.shape[2]
    col_width = pairs.shape[3]
    energies = lax.dynamic_index_in_dim(val_energy, slab[0], 0, keepdims=False)
    slots = jnp.arange(slot_count, dtype=jnp.int32)
    live = (slots[None, :] < band_counts[:, None]).reshape(-1)
    weight = jnp.where(
        live[None, :], 2.0 / (energies[:, None] - cond_energy[None, :]), jnp.float32(0.0)
    )
    blocked = pairs.reshape(n_gvec, ratio, local_v, slot_count, col_width)
    by_block = lax.all_to_all(blocked, "gvec", split_axis=0, concat_axis=2, tiled=True)
    rows_all = lax.all_gather(by_block, "band", axis=3, tiled=True)[0]
    by_column = lax.all_to_all(pairs, "band", split_axis=0, concat_axis=2, tiled=True)
    cols_all = lax.all_gather(by_column, "gvec", axis=1, tiled=True)[0]
    scaled = (weight[:, :, None] * cols_all.astype(jnp.float32)).astype(jnp.bfloat16)
    result = lax.dot_general(
        rows_all, scaled, (((1, 2), (0, 1)), ((), ())), preferred_element_type=jnp.float32
    )
    return result.reshape(ratio * col_width, col_width)


def solution(mesh):
    in_specs = (P(None, "gvec", "band", None), P(), P(), P(), P())
    out_specs = P("gvec", "band")
    return jax.shard_map(
        on_device, mesh=mesh, in_specs=in_specs, out_specs=out_specs, check_vma=False
    )
```

profile of v0, /device:TPU:1, one launch (start us, length us, event | category | flops | bytes accessed | tf_op | source)
XLA Modules:
  0.0 263.4 jit_solution(6837848196494836438)
XLA Ops:
  6.5 0.0 copy-start
  6.5 0.0 all-gather.6.cloned.1.call-start
  6.5 17.7 %all_to_all.30 = bf16[8,4,1,16,640]{4,3,2,1,0:T(8,128)(2,1)S(1)} all-to-all(bf16[8,4,1,16,640]{4,3,2,1,0:T(8,128)(2,1)} %bitcast.24), channel_id=1, replica_groups=mesh['band'=32,'gvec'=8] {'gvec'}, dimensions={0} | all-to-all | bytes 1310720 | tf_op jit(solution)/shard_map/all_to_all | solution.py:21
  24.3 1.2 copy.8
  25.5 0.0 all-gather.6.cloned.1.call-update
  25.5 0.0 all-gather.4.cloned.1.call-start
  25.6 32.6 %all_to_all.31 = bf16[32,1,16,640]{3,2,1,0:T(8,128)(2,1)} all-to-all(bf16[32,1,16,640]{3,2,1,0:T(8,128)(2,1)} %param.5), channel_id=1, replica_groups=mesh['band'=32,'gvec'=8] {'band'}, dimensions={0} | all-to-all | bytes 1310720 | tf_op jit(solution)/shard_map/all_to_all | solution.py:23
  58.2 0.0 all-gather.4.cloned.1.call-update
  58.8 0.7 iota_compare_fusion
  59.6 0.1 lt.27
  59.7 0.0 copy-done
  59.7 0.2 dynamic-slice_reduce_fusion
  59.8 0.8 divide_select_fusion
  60.6 133.8 %all-gather.6.cloned.1.call-done = bf16[1,4,8,1,512,640]{5,2,3,1,0,4:T(8,128)(2,1)} async-done(((bf16[1,4,8,1,16,640]{5,2,3,1,0,4:T(8,128)(2,1)}), bf16[1,4,8,1,512,640]{5,2,3,1,0,4:T(8,128)(2,1)}) %all-gather.6.cloned.1.call-update) | async-done | bytes 20971536 | tf_op jit(solution)/shard_map/all_gather | solution.py:22
  194.4 30.2 %copy.9 = bf16[1,4,8,1,512,640]{4,5,2,1,3,0:T(8,128)(2,1)} copy(bf16[1,4,8,1,512,640]{5,2,3,1,0,4:T(8,128)(2,1)} %all-gather.6.cloned.1.call-done) | data formatting | bytes 41943040 | tf_op jit(solution)/shard_map/all_gather | solution.py:22
  224.6 8.6 %all-gather.4.cloned.1.call-done = bf16[1,8,512,640]{3,2,0,1:T(8,128)(2,1)} async-done(((bf16[1,1,512,640]{3,2,0,1:T(8,128)(2,1)}), bf16[1,8,512,640]{3,2,0,1:T(8,128)(2,1)}) %all-gather.4.cloned.1.call-update) | async-done | bytes 5242896 | tf_op jit(solution)/shard_map/all_gather | solution.py:24
  233.3 23.3 %fusion = f32[640,4,640,1]{0,2,3,1:T(8,128)} fusion(bf16[1,4,8,1,512,640]{4,5,2,1,3,0:T(8,128)(2,1)} %copy.9, bf16[1,8,512,640]{3,2,0,1:T(8,128)(2,1)} %all-gather.4.cloned.1.call-done, f32[8,512]{1,0:T(8,128)S(1)} %divide_select_fusion), kind=kOutput, calls=%fused_computation | convolution fusion | flops 13429637120 | bytes 32784384 | tf_op jit(solution)/shard_map/dot_general | solution.py:26
Async XLA Ops:
  6.5 53.1 %copy-start = (f32[32,8]{0,1:T(8,128)S(1)}, f32[32,8]{0,1:T(8,128)}, u32[]{:S(2)}) copy-start(f32[32,8]{0,1:T(8,128)} %param.7) | copy-start | bytes 3076
  6.5 187.9 %all-gather.6.cloned.1.call-start = ((), (), s32[]{:S(2)}) async-start(), calls=%async_computation.3 | async-start | bytes 21626880 | tf_op jit(solution)/shard_map/all_gather | solution.py:22
  25.5 207.7 %all-gather.4.cloned.1.call-start = ((), (), s32[]{:S(2)}) async-start(), calls=%async_computation.2 | async-start | bytes 5898240 | tf_op jit(solution)/shard_map/all_gather | solution.py:24
Sparse Core Ops, SparseCore 0:
  25.6 168.7 all-gather.5
  196.3 36.9 all-gather.3
where the time goes:
time: 264 us; the launch traced here: 263 us
  waiting for transfers between devices  142 us (54%)
  blocking collectives  50.3 us (19%)
  local copies, waits for them, and re-layouts  31.7 us (12%)
  matrix products  23.3 us (9%)
  between operations  14.1 us (5%)
    all_gather x1, waiting for transfers between devices, on_device(): rows_all = lax.all_gather(by_block, 'band', axis=3, tiled=True)[0]  134 us
    all_to_all x1, blocking collectives, on_device(): lax.all_to_all(pairs, 'band', split_axis=0, concat_axis=2, tiled=True)  32.6 us
    all_gather x1, local copies, waits for them, and re-layouts, on_device(): rows_all = lax.all_gather(by_block, 'band', axis=3, tiled=True)[0]  30.2 us
    dot_general x1, matrix products, on_device(): lax.dot_general(rows_all, scaled, (((1, 2), (0, 1)), ((), ())), preferred...  23.3 us
    all_to_all x1, blocking collectives, on_device(): lax.all_to_all(blocked, 'gvec', split_axis=0, concat_axis=2, tiled=True)  17.7 us
    all_gather x1, waiting for transfers between devices, on_device(): cols_all = lax.all_gather(by_column, 'gvec', axis=1, tiled=True)[0]  8.62 us
  transfers between devices with their start and end apart: 2, of which 2 were waited for; matrix products, arithmetic and copies ran while one was open for 12% of the time, Pallas kernels for 0%

commit v1 on v0

--- a/solution.py
+++ b/solution.py
@@ -2,6 +2,22 @@
 import jax.numpy as jnp
 from jax import lax
 from jax.sharding import PartitionSpec as P
+
+
+def test_files(values, where_dim, xs):
+    x_next = values.shape
+    seen_now = values.reshape(
+        *x_next[:where_dim], xs, x_next[where_dim] // xs, *x_next[where_dim + 1 :]
+    )
+    mixed_arr = jnp.moveaxis(seen_now, where_dim, 0)
+    return mixed_arr
+
+
+def connect_halves_here(mat, dimension_no):
+    e_now = list(mat.shape[1:])
+    e_now[dimension_no] *= mat.shape[0]
+    low = jnp.moveaxis(mat, 0, dimension_no).reshape(e_now)
+    return low
 
 
 def on_device(pairs, cond_energy, val_energy, band_counts, slab):
@@ -18,7 +34,17 @@
         live[None, :], 2.0 / (energies[:, None] - cond_energy[None, :]), jnp.float32(0.0)
     )
     blocked = pairs.reshape(n_gvec, ratio, local_v, slot_count, col_width)
-    by_block = lax.all_to_all(blocked, "gvec", split_axis=0, concat_axis=2, tiled=True)
+    field_out = lax.axis_size("gvec")
+    then, base_arr = (field_out, lax.axis_index("gvec"))
+    last = test_files(blocked, 0, then)
+    inbox = [last[base_arr]]
+    for p in tuple(range(1, then)):
+        w2 = last[base_arr ^ p]
+        carry_out = lax.ppermute(w2, "gvec", perm=[(dev_j, dev_j ^ p) for dev_j in range(then)])
+        inbox.append(carry_out)
+    part_now = jnp.stack(inbox, 0)
+    last = part_now[base_arr ^ jnp.arange(then)]
+    by_block = connect_halves_here(last, 2)
     rows_all = lax.all_gather(by_block, "band", axis=3, tiled=True)[0]
     by_column = lax.all_to_all(pairs, "band", split_axis=0, concat_axis=2, tiled=True)
     cols_all = lax.all_gather(by_column, "gvec", axis=1, tiled=True)[0]

time: 264 us -> 266 us (level)
  blocking collectives: 50.3 us -> 34 us
  starting transfers between devices: 0.04 us -> 11.5 us
  waiting for transfers between devices: 142 us -> 149 us
    all_gather x1 -> x0, local copies, waits for them, and re-layouts: 30.2 us -> none  [on_device(): rows_all = lax.all_gather(by_block, 'band', axis=3, tiled=True)[0]]
    dot_general x0 -> x1, local copies, waits for them, and re-layouts: none -> 29 us  [on_device(): lax.dot_general(rows_all, scaled, (((1, 2), (0, 1)), ((), ())), preferred...]
    all_to_all x1 -> x0, blocking collectives: 17.7 us -> none  [on_device(): lax.all_to_all(blocked, 'gvec', split_axis=0, concat_axis=2, tiled=True)]
    ppermute x0 -> x7, starting transfers between devices: none -> 11.4 us  [on_device(): lax.ppermute(w2, 'gvec', perm=[(dev_j, dev_j ^ p) for dev_j in range(then)])]
    ppermute x0 -> x7, waiting for transfers between devices: none -> 5.68 us  [on_device(): lax.ppermute(w2, 'gvec', perm=[(dev_j, dev_j ^ p) for dev_j in range(then)])]
  transfers between devices with their start and end apart: 2 -> 9, of which waited for: 2 -> 5; matrix products, arithmetic and copies ran while one was open for 12% -> 12% of each run, Pallas kernels for 0% -> 0%
where the time goes in v1:
time: 266 us; the launch traced here: 265 us
  waiting for transfers between devices  149 us (56%)
  blocking collectives  34 us (13%)
  local copies, waits for them, and re-layouts  32.1 us (12%)
  matrix products  23.1 us (9%)
  between operations  14.1 us (5%)
  starting transfers between devices  11.5 us (4%)
    all_gather x1, waiting for transfers between devices, on_device(): rows_all = lax.all_gather(by_block, 'band', axis=3, tiled=True)[0]  133 us
    all_to_all x1, blocking collectives, on_device(): lax.all_to_all(pairs, 'band', split_axis=0, concat_axis=2, tiled=True)  34 us
    dot_general x1, local copies, waits for them, and re-layouts, on_device(): lax.dot_general(rows_all, scaled, (((1, 2), (0, 1)), ((), ())), preferred...  29 us
    dot_general x1, matrix products, on_device(): lax.dot_general(rows_all, scaled, (((1, 2), (0, 1)), ((), ())), preferred...  23.1 us
    ppermute x7, starting transfers between devices, on_device(): lax.ppermute(w2, 'gvec', perm=[(dev_j, dev_j ^ p) for dev_j in range(then)])  11.4 us
    all_gather x1, waiting for transfers between devices, on_device(): cols_all = lax.all_gather(by_column, 'gvec', axis=1, tiled=True)[0]  9.81 us
    ppermute x7, waiting for transfers between devices, on_device(): lax.ppermute(w2, 'gvec', perm=[(dev_j, dev_j ^ p) for dev_j in range(then)])  5.68 us
  transfers between devices with their start and end apart: 9, of which 5 were waited for; matrix products, arithmetic and copies ran while one was open for 12% of the time, Pallas kernels for 0%

profile of v1, /device:TPU:1, one launch (start us, length us, event | category | flops | bytes accessed | tf_op | source)
XLA Modules:
  0.0 264.8 jit_solution(14701912889824904717)
XLA Ops:
  6.5 0.0 copy-start
  6.5 0.0 all-gather.6.cloned.1.call-start
  6.5 1.2 dynamic-slice_bitcast_fusion
  7.8 3.3 %collective-permute-start = (bf16[1,4,1,16,640]{4,3,1,2,0:T(8,128)(2,1)S(1)}, bf16[1,4,1,16,640]{4,3,1,2,0:T(8,128)(2,1)S(1)}, u32[]{:S(2)}, u32[]{:S(2)}) collective-permute-start(bf16[1,4,1,16,640]{4,3,1,2,0:T(8,128)(2,1)S(1)} %get-tuple-element.11), channel_id=1, source_target_pairs={{0,1},{1,0},{2,3},{3,2},{4,5},{5,4},{6,7},{7,6},{8,9},{9,8},{10,11... | collective-permute-start | bytes 245768 | tf_op jit(solution)/shard_map/ppermute | solution.py:43
  11.1 0.0 collective-permute-start.1
  11.1 1.7 collective-permute-start.2
  12.8 1.2 collective-permute-start.3
  14.0 2.1 collective-permute-start.4
  16.1 0.0 collective-permute-done
  16.2 1.1 collective-permute-start.5
  17.3 0.0 collective-permute-done.1
  17.3 2.0 collective-permute-start.6
  19.3 0.0 collective-permute-done.2
  19.3 0.0 collective-permute-done.3
  19.3 2.0 collective-permute-done.4
  21.4 1.9 collective-permute-done.5
  23.3 1.7 collective-permute-done.6
  25.0 1.5 gather_fusion
  26.5 0.0 all-gather.6.cloned.1.call-update
  26.5 0.0 all-gather.4.cloned.1.call-start
  26.6 34.0 %all_to_all.12 = bf16[32,1,16,640]{3,2,1,0:T(8,128)(2,1)} all-to-all(bf16[32,1,16,640]{3,2,1,0:T(8,128)(2,1)} %param.5), channel_id=1, replica_groups=mesh['band'=32,'gvec'=8] {'band'}, dimensions={0} | all-to-all | bytes 1310720 | tf_op jit(solution)/shard_map/all_to_all | solution.py:49
  60.6 0.0 all-gather.4.cloned.1.call-update
  61.3 0.7 iota_compare_fusion
  62.0 0.1 lt.70
  62.1 0.0 copy-done
  62.1 0.2 dynamic-slice_reduce_fusion
  62.3 0.8 divide_select_fusion
  63.0 133.0 %all-gather.6.cloned.1.call-done = bf16[1,4,8,1,512,640]{5,4,1,2,3,0:T(8,128)(2,1)} async-done(((bf16[1,4,8,1,16,640]{5,4,1,2,3,0:T(8,128)(2,1)}), bf16[1,4,8,1,512,640]{5,4,1,2,3,0:T(8,128)(2,1)}) %all-gather.6.cloned.1.call-update) | async-done | bytes 20971536 | tf_op jit(solution)/shard_map/all_gather | solution.py:48
  196.0 29.0 %copy.7 = bf16[4,640,8,512]{3,1,0,2:T(8,128)(2,1)} copy(bf16[4,640,8,512]{1,3,0,2:T(8,128)(2,1)} %bitcast.50) | data formatting | bytes 41943040 | tf_op jit(solution)/shard_map/dot_general | solution.py:52
  225.1 9.8 %all-gather.4.cloned.1.call-done = bf16[1,8,512,640]{3,2,0,1:T(8,128)(2,1)} async-done(((bf16[1,1,512,640]{3,2,0,1:T(8,128)(2,1)}), bf16[1,8,512,640]{3,2,0,1:T(8,128)(2,1)}) %all-gather.4.cloned.1.call-update) | async-done | bytes 5242896 | tf_op jit(solution)/shard_map/all_gather | solution.py:50
  234.9 23.1 %convolution_bitcast_fusion = f32[2560,640]{1,0:T(8,128)} fusion(bf16[2560,8,512]{2,0,1:T(8,128)(2,1)} %bitcast.51, bf16[1,8,512,640]{3,2,0,1:T(8,128)(2,1)} %all-gather.4.cloned.1.call-done, f32[8,512]{1,0:T(8,128)S(1)} %divide_select_fusion), kind=kOutput, calls=%fused_computation.2 | convolution fusion | flops 13429637120 | bytes 32784384 | tf_op jit(solution)/shard_map/dot_general | solution.py:52
  (9 shorter events, 0.1 us)
Async XLA Ops:
  6.5 55.6 %copy-start = (f32[32,8]{0,1:T(8,128)S(1)}, f32[32,8]{0,1:T(8,128)}, u32[]{:S(2)}) copy-start(f32[32,8]{0,1:T(8,128)} %param.7) | copy-start | bytes 3076
  6.5 189.5 %all-gather.6.cloned.1.call-start = ((), (), s32[]{:S(2)}) async-start(), calls=%async_computation.2 | async-start | bytes 21626880 | tf_op jit(solution)/shard_map/all_gather | solution.py:48
  7.8 8.4 %collective-permute-start = (bf16[1,4,1,16,640]{4,3,1,2,0:T(8,128)(2,1)S(1)}, bf16[1,4,1,16,640]{4,3,1,2,0:T(8,128)(2,1)S(1)}, u32[]{:S(2)}, u32[]{:S(2)}) collective-permute-start(bf16[1,4,1,16,640]{4,3,1,2,0:T(8,128)(2,1)S(1)} %get-tuple-element.11), channel_id=1, source_target_pairs={{0,1},{1,0},{2,3},{3,2},{4,5},{5,4},{6,7},{7,6},{8,9},{9,8},{10,11... | collective-permute-start | bytes 245768 | tf_op jit(solution)/shard_map/ppermute | solution.py:43
  11.1 6.2 %collective-permute-start.1 = (bf16[1,4,1,16,640]{4,3,1,2,0:T(8,128)(2,1)S(1)}, bf16[1,4,1,16,640]{4,3,1,2,0:T(8,128)(2,1)S(1)}, u32[]{:S(2)}, u32[]{:S(2)}) collective-permute-start(bf16[1,4,1,16,640]{4,3,1,2,0:T(8,128)(2,1)S(1)} %get-tuple-element.10), channel_id=1, source_target_pairs={{0,2},{1,3},{2,0},{3,1},{4,6},{5,7},{6,4},{7,5},{8,10},{9,11},{10,... | collective-permute-start | bytes 245768 | tf_op jit(solution)/shard_map/ppermute | solution.py:43
  11.1 8.2 %collective-permute-start.2 = (bf16[1,4,1,16,640]{4,3,1,2,0:T(8,128)(2,1)S(1)}, bf16[1,4,1,16,640]{4,3,1,2,0:T(8,128)(2,1)S(1)}, u32[]{:S(2)}, u32[]{:S(2)}) collective-permute-start(bf16[1,4,1,16,640]{4,3,1,2,0:T(8,128)(2,1)S(1)} %get-tuple-element.9), channel_id=1, source_target_pairs={{0,3},{1,2},{2,1},{3,0},{4,7},{5,6},{6,5},{7,4},{8,11},{9,10},{10,... | collective-permute-start | bytes 245768 | tf_op jit(solution)/shard_map/ppermute | solution.py:43
  12.8 6.5 %collective-permute-start.3 = (bf16[1,4,1,16,640]{4,3,1,2,0:T(8,128)(2,1)S(1)}, bf16[1,4,1,16,640]{4,3,1,2,0:T(8,128)(2,1)S(1)}, u32[]{:S(2)}, u32[]{:S(2)}) collective-permute-start(bf16[1,4,1,16,640]{4,3,1,2,0:T(8,128)(2,1)S(1)} %get-tuple-element.8), channel_id=1, source_target_pairs={{0,4},{1,5},{2,6},{3,7},{4,0},{5,1},{6,2},{7,3},{8,12},{9,13},{10,... | collective-permute-start | bytes 245768 | tf_op jit(solution)/shard_map/ppermute | solution.py:43
  14.0 7.4 %collective-permute-start.4 = (bf16[1,4,1,16,640]{4,3,1,2,0:T(8,128)(2,1)S(1)}, bf16[1,4,1,16,640]{4,3,1,2,0:T(8,128)(2,1)S(1)}, u32[]{:S(2)}, u32[]{:S(2)}) collective-permute-start(bf16[1,4,1,16,640]{4,3,1,2,0:T(8,128)(2,1)S(1)} %get-tuple-element.7), channel_id=1, source_target_pairs={{0,5},{1,4},{2,7},{3,6},{4,1},{5,0},{6,3},{7,2},{8,13},{9,12},{10,... | collective-permute-start | bytes 245768 | tf_op jit(solution)/shard_map/ppermute | solution.py:43
  16.2 7.1 %collective-permute-start.5 = (bf16[1,4,1,16,640]{4,3,1,2,0:T(8,128)(2,1)S(1)}, bf16[1,4,1,16,640]{4,3,1,2,0:T(8,128)(2,1)S(1)}, u32[]{:S(2)}, u32[]{:S(2)}) collective-permute-start(bf16[1,4,1,16,640]{4,3,1,2,0:T(8,128)(2,1)S(1)} %get-tuple-element.6), channel_id=1, source_target_pairs={{0,6},{1,7},{2,4},{3,5},{4,2},{5,3},{6,0},{7,1},{8,14},{9,15},{10,... | collective-permute-start | bytes 245768 | tf_op jit(solution)/shard_map/ppermute | solution.py:43
  17.3 7.8 %collective-permute-start.6 = (bf16[1,4,1,16,640]{4,3,1,2,0:T(8,128)(2,1)S(1)}, bf16[1,4,1,16,640]{4,3,1,2,0:T(8,128)(2,1)S(1)}, u32[]{:S(2)}, u32[]{:S(2)}) collective-permute-start(bf16[1,4,1,16,640]{4,3,1,2,0:T(8,128)(2,1)S(1)} %get-tuple-element.5), channel_id=1, source_target_pairs={{0,7},{1,6},{2,5},{3,4},{4,3},{5,2},{6,1},{7,0},{8,15},{9,14},{10,... | collective-permute-start | bytes 245768 | tf_op jit(solution)/shard_map/ppermute | solution.py:43
  26.5 208.3 %all-gather.4.cloned.1.call-start = ((), (), s32[]{:S(2)}) async-start(), calls=%async_computation.1 | async-start | bytes 5898240 | tf_op jit(solution)/shard_map/all_gather | solution.py:50
Sparse Core Ops, SparseCore 0:
  26.7 169.3 all-gather.5
  197.9 36.9 all-gather.3
